TPU v7x, 128 devices: a whole 4x4x4 slice. The times are simulated.
128 devices in a mesh: psg: 8 (over y_lo, x), head: 16 (over y_hi, z, core).
Axes of the slice: x: 4, y: 4 (y_hi: 2, y_lo: 2; y = y_hi * 2 + y_lo), z: 4, core: 2. Of those that a mesh axis runs over, the one named last changes fastest.
Arguments:
- queries: bfloat16 [256, 4096], P(None, 'head'), may hold values from -16 to 16
- memory: bfloat16 [8192, 4096], P('psg', 'head'), may hold values from -6 to 6
- lengths: int32 [32], P('psg'), may hold values from 32 to 256
- owner: int32 [32], P('psg'), may hold values from 0 to 1, as said below
- w_key: bfloat16 [4096, 4096], P(None, 'head'), may hold values from -0.09375 to 0.09375
- w_value: bfloat16 [4096, 4096], P(None, 'head'), may hold values from -0.09375 to 0.09375
- grad_context: bfloat16 [256, 4096], P(None, 'head'), may hold values from -6 to 6
Outputs:
- grad_queries: bfloat16 [256, 4096], P(None, 'head')
- grad_memory: bfloat16 [8192, 4096], P('psg', 'head')
- grad_wk: float32 [4096, 4096], P('psg', 'head')
- grad_wv: float32 [4096, 4096], P('psg', 'head')
Inputs may be any that keep to these rules, and one draw needn't show every extreme that they name: `owner`: each question owns exactly 16 passages.
All inputs are finite; a program needn't handle non-finite values.
Results may differ from a plain program's by a relative error of at most 0.022.
The roundings to bfloat16 on the way count: a program that leaves them out, or rounds other values in their place, can miss the bound.
Values may be sent and summed in bfloat16 or wider, within the bound.
A program may use at most 128 MiB of HBM per device.

v0:
```python
import jax
import jax.numpy as jnp
from jax import lax
from jax.experimental import pallas as pl
from jax.experimental.pallas import tpu as pltpu
from jax.sharding import PartitionSpec as P

HEAD_DIM = 64
LEN = 256
TQ = 128
HEADS_HERE = 4
PASSAGES_HERE = 4
B = 256
PAIRS = HEADS_HERE * TQ
MESH = pl.DeviceIdType.MESH
FILL = -1e30
F32 = jnp.float32
BF16 = jnp.bfloat16

PLACES = ((0, 0), (0, 1), (0, 3), (1, 0), (0, 2), (1, 2), (1, 1), (1, 3))
SLOT = {place: slot for slot, place in enumerate(PLACES)}


def is_equal(a, k):
    return 1 - ((a - k) * (a - k) + 48) // 49


def slot_of(dy, dz):
    code = dy * 4 + dz
    total = 0
    for (py, pz), slot in SLOT.items():
        total = total + slot * is_equal(code, py * 4 + pz)
    return total


def nt(a, b):
    return lax.dot_general(a, b, (((1,), (1,)), ((), ())), preferred_element_type=F32)


def nn(a, b):
    return jnp.dot(a, b, preferred_element_type=F32)


class Scatter:
    def __init__(self, send, recv, ysend, yrecv, ssem, rsem, yssem, yrsem, following, before, partner):
        self.send, self.recv, self.ysend, self.yrecv = send, recv, ysend, yrecv
        self.ssem, self.rsem, self.yssem, self.yrsem = ssem, rsem, yssem, yrsem
        self.following, self.before, self.partner = following, before, partner

    def half(self, ref, index, way):
        return ref.at[index, pl.ds(way * B, B)]

    def copy(self, index, way):
        return pltpu.make_async_remote_copy(
            src_ref=self.half(self.send, index, way),
            dst_ref=self.half(self.recv, index, way),
            send_sem=self.ssem.at[index, way],
            recv_sem=self.rsem.at[index, way],
            device_id=self.before if way else self.following,
            device_id_type=MESH,
        )

    def ycopy(self, u):
        return pltpu.make_async_remote_copy(
            src_ref=self.ysend.at[u],
            dst_ref=self.yrecv.at[u],
            send_sem=self.yssem.at[u],
            recv_sem=self.yrsem.at[u],
            device_id=self.partner,
            device_id_type=MESH,
        )

    def arrived(self, index, way):
        return self.recv[index, way * B : (way + 1) * B, :].astype(F32)

    def item(self, kind, dy, u, own, store):
        first = (dy * 2 + u) * 3
        if kind == "D":
            mine = [own(0, way * 2 + u, way) for way in (0, 1)]
            for way in (0, 1):
                self.copy(first + 1, way).wait_recv()
                self.copy(first + 2, way).wait_recv()
            if dy == 0:
                self.ycopy(u).wait_recv()
            for way in (0, 1):
                value = mine[way] + self.arrived(first + 2, way) + self.arrived(first + 1, 1 - way)
                if dy == 1:
                    self.ysend[u, way * B : (way + 1) * B, :] = value.astype(BF16)
                else:
                    value = value + self.yrecv[u, way * B : (way + 1) * B, :].astype(F32)
                    store(way * 2 + u, value)
            if dy == 1:
                self.ycopy(u).start()
            return
        index = first + "ABC".index(kind)
        for way in (0, 1):
            dz, r = chunk_of(kind, u, way)
            value = own(dz, r, way)
            if kind == "C":
                self.copy(first, way).wait_recv()
                value = value + self.arrived(first, way)
            self.send[index, way * B : (way + 1) * B, :] = value.astype(BF16)
            self.copy(index, way).start()

    def finish(self, indices):
        for index in indices:
            for way in (0, 1):
                self.copy(index, way).wait_send()

    def finish_y(self):
        for u in (0, 1):
            self.ycopy(u).wait_send()


def chunk_of(kind, u, way):
    if kind == "A":
        return 2, way * 2 + u
    if kind == "B":
        return (3, u) if way else (1, 2 + u)
    if kind == "C":
        return (3, 2 + u) if way else (1, u)
    return 0, way * 2 + u


ITEMS = (
    ("A", 1, 0), ("B", 1, 0), ("C", 1, 0), ("A", 1, 1), ("B", 1, 1), ("D", 1, 0),
    ("C", 1, 1), ("A", 0, 0), ("B", 0, 0), ("D", 1, 1), ("C", 0, 0), ("A", 0, 1),
    ("B", 0, 1), ("C", 0, 1), ("D", 0, 0), ("D", 0, 1),
)
LAST = (4, 5)
EARLIER = tuple(index for index in range(12) if index not in LAST)


def kernel(
    len_ref, own_ref, q_in, c_in, mem_ref, wk_ref, wv_ref,
    gq_out, gm_out, gw_out,
    q_ref, c_ref, gm_own, gw_own, fm, w, qa, ca, qat, cat, acc, kt, e_ref, gp_ref, stat, sl, sall, g, gt, gs,
    sib_send, sib_recv, m_send, m_recv, my_send, my_recv, w_send, w_recv, wy_send, wy_recv,
    gq_acc, gq_send, gq_recv, gq_own, gq_full,
    mem_sem, w_sem, qc_sem, out_sem, ag_ssem, ag_rsem, st_ssem, st_rsem, sib_ssem, sib_rsem,
    m_ssem, m_rsem, my_ssem, my_rsem, w_ssem, w_rsem, wy_ssem, wy_rsem,
    q1_ssem, q1_rsem, q2_ssem, q2_rsem,
):
    p, h = lax.axis_index("psg"), lax.axis_index("head")
    yl, x = p // 4, p % 4
    yh, z, core = h // 8, (h // 2) % 4, h % 2

    def head_at(dy, dz, dc=0):
        return ((yh + dy) % 2) * 8 + ((z + dz) % 4) * 2 + (core + dc) % 2

    def psg_at(dy, dx):
        return ((yl + dy) % 2) * 4 + (x + dx) % 4

    def on_head(dy, dz, dc=0):
        return (p, head_at(dy, dz, dc))

    def on_psg(dy, dx):
        return (psg_at(dy, dx), h)

    up, down, across, sibling = on_head(0, 1), on_head(0, 3), on_head(1, 0), on_head(0, 0, 1)
    peers = [(k // 4, k % 4) for k in range(1, 8)]

    mem_copy = pltpu.make_async_copy(mem_ref, fm.at[:, pl.ds(0, B)], mem_sem)
    mem_copy.start()
    q_copies = [
        pltpu.make_async_copy(q_in, q_ref, qc_sem.at[0]),
        pltpu.make_async_copy(c_in, c_ref, qc_sem.at[1]),
    ]
    for copy in q_copies:
        copy.start()
    barrier = pltpu.get_barrier_semaphore()
    partners = [on_psg(*peer) for peer in reversed(peers)] + [across, up, down, sibling]
    for device in partners:
        pl.semaphore_signal(barrier, inc=1, device_id=device, device_id_type=MESH)
    pl.semaphore_wait(barrier, len(partners))

    def block(slot, dc, r):
        return fm.at[pl.ds(r * B, B), pl.ds((slot * 2 + dc) * B, B)]

    def gather_copy(source, target, r, number, device):
        return pltpu.make_async_remote_copy(
            src_ref=block(source[0], source[1], r),
            dst_ref=block(target[0], target[1], r),
            send_sem=ag_ssem.at[number, r],
            recv_sem=ag_rsem.at[target[0] * 2 + target[1], r],
            device_id=device,
            device_id_type=MESH,
        )

    def gathered(slot, dc, r):
        gather_copy((slot, dc), (slot, dc), r, 0, sibling).wait_recv()

    def to_sibling(slot, r):
        gather_copy((slot, 0), (slot, 1), r, 4 + slot, sibling).start()

    def own_copy(target, r, number, device):
        return pltpu.make_async_remote_copy(
            src_ref=mem_ref.at[pl.ds(r * B, B)],
            dst_ref=block(target, 0, r),
            send_sem=ag_ssem.at[number, r],
            recv_sem=ag_rsem.at[target * 2, r],
            device_id=device,
            device_id_type=MESH,
        )

    def own_along(k):
        own_copy(SLOT[0, 3], k, 0, up).start()
        own_copy(SLOT[0, 1], (k + 2) % 4, 1, down).start()

    own_along(0)
    own_along(1)
    for k in range(PASSAGES_HERE):
        own_copy(SLOT[1, 0], k % 2 * 2 + k // 2, 2, across).start()
    mem_copy.wait()
    for r in range(PASSAGES_HERE):
        to_sibling(0, r)
    w_copies = []
    for slot, (dy, dz) in enumerate(PLACES):
        for dc in (0, 1):
            rows = pl.ds(pl.multiple_of(head_at(dy, dz, dc) * B, B), B)
            into = pl.ds((slot * 2 + dc) * B, B)
            for part, ref in enumerate((wk_ref, wv_ref)):
                w_copies.append(
                    pltpu.make_async_copy(
                        ref.at[rows, :],
                        w.at[into, pl.ds(part * B, B)],
                        w_sem.at[(slot * 2 + dc) * 2 + part],
                    )
                )
                w_copies[-1].start()

    def opposite(r):
        gathered(SLOT[0, 2], 0, r)
        gather_copy((SLOT[0, 2], 0), (SLOT[1, 2], 0), r, 14, across).start()
        to_sibling(SLOT[0, 2], r)

    def partner(r):
        gathered(SLOT[1, 0], 0, r)
        gather_copy((SLOT[1, 0], 0), (SLOT[1, 3], 0), r, 12, up).start()
        gather_copy((SLOT[1, 0], 0), (SLOT[1, 1], 0), r, 13, down).start()
        to_sibling(SLOT[1, 0], r)

    for r in (0, 1):
        gathered(SLOT[0, 3], 0, r)
        gather_copy((SLOT[0, 3], 0), (SLOT[0, 2], 0), r, 3, up).start()
        gathered(SLOT[0, 1], 0, 2 + r)
        gather_copy((SLOT[0, 1], 0), (SLOT[0, 2], 0), 2 + r, 3, down).start()
        own_along(2 + r)
        to_sibling(SLOT[0, 3], r)
        to_sibling(SLOT[0, 1], 2 + r)
    for r in (0, 1):
        partner(r)
        partner(2 + r)
        opposite(r)
        opposite(2 + r)

    lane = lax.broadcasted_iota(jnp.int32, (TQ, B), 1) // HEAD_DIM
    row = lax.broadcasted_iota(jnp.int32, (B, TQ), 0) // HEAD_DIM
    for copy in q_copies:
        copy.wait()
    for source, plain, turned in ((q_ref, qa, qat), (c_ref, ca, cat)):
        for question in range(2):
            mine = source[question * TQ : (question + 1) * TQ, :].astype(F32)
            mine_t = mine.T
            for head in range(HEADS_HERE):
                at = slice(head * TQ, (head + 1) * TQ)
                plain[question, at, :] = jnp.where(lane == head, mine, 0.0).astype(BF16)
                turned[question, :, at] = jnp.where(row == head, mine_t, 0.0).astype(BF16)

    def rows_of(r):
        return pl.ds(pl.multiple_of(r * B, B), B)

    def passage(k):
        return k % 2 * 2 + k // 2

    for r in (0, 1):
        gathered(SLOT[0, 1], 0, r)
        to_sibling(SLOT[0, 1], r)
        gathered(SLOT[0, 3], 0, 2 + r)
        to_sibling(SLOT[0, 3], 2 + r)

    for copy in w_copies[:16]:
        copy.wait()

    def first_part(k, carry):
        r = passage(k)
        for slot in range(4):
            gathered(slot, 1, r)
        acc[rows_of(r), :] = nn(fm[rows_of(r), 0 : 8 * B], w[0 : 8 * B, :])
        return carry

    lax.fori_loop(0, PASSAGES_HERE, first_part, 0)

    for copy in w_copies[16:]:
        copy.wait()

    def second_part(k, carry):
        @pl.when(k < PASSAGES_HERE)
        def _():
            r = passage(k)
            for slot in (SLOT[1, 2], SLOT[1, 1], SLOT[1, 3]):
                gathered(slot, 0, r)
                to_sibling(slot, r)
            gathered(SLOT[0, 2], 1, r)
            gathered(SLOT[1, 2], 1, r)
            acc[rows_of(r), :] += nn(fm[rows_of(r), 8 * B : 12 * B], w[8 * B : 12 * B, :])

        @pl.when(k > 0)
        def _():
            attend(passage(k - 1))

        return carry

    def attend(r):
        for slot in (SLOT[1, 1], SLOT[1, 3]):
            gathered(slot, 1, r)
        both = acc[rows_of(r), :] + nn(fm[rows_of(r), 12 * B :], w[12 * B :, :])
        keys, values = both[:, :B], both[:, B:].astype(BF16)
        kt[r] = keys.T.astype(BF16)
        keys = keys.astype(BF16)
        question = own_ref[r]
        scores = nt(keys, qa[question])
        flows = nt(values, ca[question])
        alive = lax.broadcasted_iota(jnp.int32, (LEN, PAIRS), 0) < len_ref[r]
        masked = jnp.where(alive, scores, FILL)
        top = jnp.max(masked, axis=0, keepdims=True)
        shifted = jnp.where(alive, jnp.exp(masked - top), 0.0)
        e_ref[r] = shifted
        gp_ref[r] = flows
        stat[r, 0:1, :] = top
        stat[r, 1:2, :] = jnp.sum(shifted, axis=0, keepdims=True)
        stat[r, 2:3, :] = jnp.sum(shifted * flows, axis=0, keepdims=True)

    lax.fori_loop(0, PASSAGES_HERE + 1, second_part, 0)

    picks = []
    for r in range(PASSAGES_HERE):
        second = own_ref[r].astype(F32)
        picks.append((1.0 - second, second))
    for question in range(2):
        tops = [
            stat[r, 0:1, :] * picks[r][question] + FILL * (1.0 - picks[r][question])
            for r in range(PASSAGES_HERE)
        ]
        top = jnp.maximum(jnp.maximum(tops[0], tops[1]), jnp.maximum(tops[2], tops[3]))
        mass = jnp.zeros((1, PAIRS), F32)
        flow = jnp.zeros((1, PAIRS), F32)
        for r in range(PASSAGES_HERE):
            scale = jnp.exp(tops[r] - top) * picks[r][question]
            mass += stat[r, 1:2, :] * scale
            flow += stat[r, 2:3, :] * scale
        sl[question : question + 1, :] = top
        sl[2 + question : 3 + question, :] = mass
        sl[4 + question : 5 + question, :] = flow
    sl[6:8, :] = jnp.zeros((2, PAIRS), F32)

    def seen_by(dy, dx):
        return dy * 4 + (4 - dx) % 4

    def stat_copy(dy, dx):
        there = seen_by(dy, dx)
        return pltpu.make_async_remote_copy(
            src_ref=sl,
            dst_ref=sall.at[there],
            send_sem=st_ssem.at[dy * 4 + dx],
            recv_sem=st_rsem.at[there],
            device_id=on_psg(dy, dx),
            device_id_type=MESH,
        )

    for peer in peers:
        stat_copy(*peer).start()
    for peer in peers:
        stat_copy(*peer).wait_recv()
    sall[0] = sl[...]
    totals = []
    for question in range(2):
        tops = [sall[k, question : question + 1, :] for k in range(8)]
        top = tops[0]
        for other in tops[1:]:
            top = jnp.maximum(top, other)
        mass = jnp.zeros((1, PAIRS), F32)
        flow = jnp.zeros((1, PAIRS), F32)
        for k in range(8):
            scale = jnp.exp(tops[k] - top)
            mass += sall[k, 2 + question : 3 + question, :] * scale
            flow += sall[k, 4 + question : 5 + question, :] * scale
        totals.append((top, 1.0 / mass, flow / mass))
    for r in range(PASSAGES_HERE):
        top, inverse, shift = (
            totals[0][k] * picks[r][0] + totals[1][k] * picks[r][1] for k in range(3)
        )
        stat[r, 3:4, :] = jnp.exp(stat[r, 0:1, :] - top) * inverse
        stat[r, 4:5, :] = shift

    def gradients(k, carry):
        r = passage(k)
        question = own_ref[r]
        probs = e_ref[r] * stat[r, 3:4, :]
        grad = (probs * (gp_ref[r] - stat[r, 4:5, :])).astype(BF16)
        probs = probs.astype(BF16)
        gs[r] = grad
        g[rows_of(r), 0:B] = nn(grad, qa[question]).astype(BF16)
        g[rows_of(r), B : 2 * B] = nn(probs, ca[question]).astype(BF16)
        gt[0:B, rows_of(r)] = nt(qat[question], grad).astype(BF16)
        gt[B : 2 * B, rows_of(r)] = nt(cat[question], probs).astype(BF16)
        return carry

    lax.fori_loop(0, 2, gradients, 0)

    over_head = Scatter(
        m_send, m_recv, my_send, my_recv, m_ssem, m_rsem, my_ssem, my_rsem, up, down, across
    )
    over_psg = Scatter(
        w_send, w_recv, wy_send, wy_recv, w_ssem, w_rsem, wy_ssem, wy_rsem,
        on_psg(0, 1), on_psg(0, 3), on_psg(1, 0),
    )

    def out_copy(source, target, number):
        return pltpu.make_async_copy(source, target, out_sem.at[number])

    def part(slot, dc, r):
        at = (slot * 2 + dc) * B
        return nt(g[r * B : (r + 1) * B, :], w[at : at + B, :]).astype(BF16)

    def sibling_copy(number):
        return pltpu.make_async_remote_copy(
            src_ref=sib_send.at[number],
            dst_ref=sib_recv.at[number],
            send_sem=sib_ssem.at[number],
            recv_sem=sib_rsem.at[number],
            device_id=sibling,
            device_id_type=MESH,
        )

    def sibling_item(number):
        kind, dy, u = ITEMS[number]
        for way in (0, 1):
            dz, r = chunk_of(kind, u, way)
            sib_send[number, way * B : (way + 1) * B, :] = part(SLOT[dy, dz], 1, r)
        sibling_copy(number).start()

    def head_item(number):
        kind, dy, u = ITEMS[number]
        sibling_copy(number).wait_recv()

        def own(dz, r, way):
            other = sib_recv[number, way * B : (way + 1) * B, :].astype(F32)
            return part(SLOT[dy, dz], 0, r).astype(F32) + other

        def store(r, value):
            gm_own[r * B : (r + 1) * B, :] = value.astype(BF16)
            out_copy(gm_own.at[pl.ds(r * B, B)], gm_out.at[pl.ds(r * B, B)], r).start()

        over_head.item(kind, dy, u, own, store)

    def psg_item(number):
        kind, dy, u = ITEMS[number]

        def own(dx, r, way):
            kv, half = r // 2, r % 2
            slot = slot_of((yl + dy + 2 - yh) % 2, (x + dx + 4 - z) % 4)
            column = (slot * 2 + (half + 2 - core) % 2) * B
            return nn(gt[kv * B : (kv + 1) * B, :], fm[:, pl.ds(pl.multiple_of(column, B), B)])

        def store(r, value):
            gw_own[r] = value
            out_copy(gw_own.at[r], gw_out.at[r], 4 + r).start()

        over_psg.item(kind, dy, u, own, store)

    piece = 2 * B // 8

    def q1_copy(dy, dx):
        there = seen_by(dy, dx)
        start = pl.multiple_of(psg_at(dy, dx) * piece, piece)
        return pltpu.make_async_remote_copy(
            src_ref=gq_send.at[pl.ds(start, piece)],
            dst_ref=gq_recv.at[there],
            send_sem=q1_ssem.at[dy * 4 + dx],
            recv_sem=q1_rsem.at[there],
            device_id=on_psg(dy, dx),
            device_id_type=MESH,
        )

    def q2_copy(dy, dx):
        return pltpu.make_async_remote_copy(
            src_ref=gq_own,
            dst_ref=gq_full.at[p],
            send_sem=q2_ssem.at[dy * 4 + dx],
            recv_sem=q2_rsem.at[seen_by(dy, dx)],
            device_id=on_psg(dy, dx),
            device_id_type=MESH,
        )

    def q2_wait(dy, dx):
        pltpu.make_async_remote_copy(
            src_ref=gq_own,
            dst_ref=gq_full.at[psg_at(dy, dx)],
            send_sem=q2_ssem.at[dy * 4 + dx],
            recv_sem=q2_rsem.at[dy * 4 + dx],
            device_id=on_psg(dy, dx),
            device_id_type=MESH,
        ).wait_recv()

    def query_terms():
        gq_acc[...] = jnp.zeros((2 * B, TQ), F32)
        for r in range(PASSAGES_HERE):
            term = nn(kt[r], gs[r])
            for head in range(HEADS_HERE):
                at = slice(head * HEAD_DIM, (head + 1) * HEAD_DIM)
                mine = term[at, head * TQ : (head + 1) * TQ]
                gq_acc[at, :] += mine * picks[r][0]
                after = slice(B + head * HEAD_DIM, B + (head + 1) * HEAD_DIM)
                gq_acc[after, :] += mine * picks[r][1]
        gq_send[...] = gq_acc[...].astype(BF16)
        for peer in peers:
            q1_copy(*peer).start()

    def query_sums():
        total = gq_acc[pl.ds(pl.multiple_of(p * piece, piece), piece), :]
        for dy, dx in peers:
            there = dy * 4 + dx
            pltpu.make_async_remote_copy(
                src_ref=gq_recv.at[there],
                dst_ref=gq_recv.at[there],
                send_sem=q1_ssem.at[there],
                recv_sem=q1_rsem.at[there],
                device_id=on_psg(dy, dx),
                device_id_type=MESH,
            ).wait_recv()
            total = total + gq_recv[there].astype(F32)
        gq_own[...] = total.astype(BF16)
        for peer in peers:
            q2_copy(*peer).start()
        gq_full[p] = gq_own[...]

    def query_end():
        for peer in peers:
            q2_wait(*peer)
        out_copy(gq_full, gq_out, 8).start()

    def gather_sent(r, carry):
        for number in range(15):
            gather_copy((0, 0), (0, 0), r, number, sibling).wait_send()
        return carry

    def sent():
        lax.fori_loop(0, PASSAGES_HERE, gather_sent, 0)
        for peer in peers:
            stat_copy(*peer).wait_send()
            q1_copy(*peer).wait_send()
            q2_copy(*peer).wait_send()
        for number in range(len(ITEMS) - 1):
            sibling_copy(number).wait_send()

    sibling_item(0)
    lax.fori_loop(2, 4, gradients, 0)
    for number in range(len(ITEMS)):
        if number == 14:
            query_end()
            sent()
            over_head.finish(EARLIER)
            over_psg.finish(EARLIER)
        psg_item(number)
        if number + 1 < len(ITEMS):
            sibling_item(number + 1)
        head_item(number)
        if number == 2:
            query_terms()
        if number == 8:
            query_sums()

    sibling_copy(len(ITEMS) - 1).wait_send()
    over_head.finish(LAST)
    over_psg.finish(LAST)
    over_head.finish_y()
    over_psg.finish_y()
    for r in range(PASSAGES_HERE):
        out_copy(gm_own.at[pl.ds(r * B, B)], gm_out.at[pl.ds(r * B, B)], r).wait()
        out_copy(gw_own.at[r], gw_out.at[r], 4 + r).wait()
    out_copy(gq_full, gq_out, 8).wait()


def epilogue(gq_in, gm_in, gw_in, gq_out, gm_out, gwk_out, gwv_out):
    gm_out[...] = gm_in[...]
    for r in range(4):
        out = gwk_out if r < 2 else gwv_out
        half = r % 2
        out[half * B : (half + 1) * B, :] = gw_in[r].T
    for question in range(2):
        turned = jnp.concatenate([gq_in[question * 4 + k] for k in range(4)], axis=0)
        gq_out[question * TQ : (question + 1) * TQ, :] = turned.astype(F32).T.astype(BF16)


def on_device(queries, memory, lengths, owner, w_key, w_value, grad_context):
    rows, width = memory.shape[0], w_key.shape[0]
    vmem = pl.BlockSpec(memory_space=pltpu.VMEM)
    smem = pl.BlockSpec(memory_space=pltpu.SMEM)
    anywhere = pl.BlockSpec(memory_space=pl.ANY)
    dma = pltpu.SemaphoreType.DMA
    half = 2 * B
    outs = pl.pallas_call(
        kernel,
        out_shape=(
            jax.ShapeDtypeStruct((8, 2 * B // 8, TQ), BF16),
            jax.ShapeDtypeStruct((rows, B), BF16),
            jax.ShapeDtypeStruct((4, B, B), F32),
        ),
        in_specs=[smem, smem] + [anywhere] * 5,
        out_specs=[anywhere] * 3,
        scratch_shapes=[
            pltpu.VMEM((2 * TQ, B), BF16),
            pltpu.VMEM((2 * TQ, B), BF16),
            pltpu.VMEM((rows, B), BF16),
            pltpu.VMEM((4, B, B), F32),
            pltpu.VMEM((rows, width), BF16),
            pltpu.VMEM((width, 2 * B), BF16),
            pltpu.VMEM((2, PAIRS, B), BF16),
            pltpu.VMEM((2, PAIRS, B), BF16),
            pltpu.VMEM((2, B, PAIRS), BF16),
            pltpu.VMEM((2, B, PAIRS), BF16),
            pltpu.VMEM((rows, 2 * B), F32),
            pltpu.VMEM((PASSAGES_HERE, B, B), BF16),
            pltpu.VMEM((PASSAGES_HERE, LEN, PAIRS), F32),
            pltpu.VMEM((PASSAGES_HERE, LEN, PAIRS), F32),
            pltpu.VMEM((PASSAGES_HERE, 8, PAIRS), F32),
            pltpu.VMEM((8, PAIRS), F32),
            pltpu.VMEM((8, 8, PAIRS), F32),
            pltpu.VMEM((rows, 2 * B), BF16),
            pltpu.VMEM((2 * B, rows), BF16),
            pltpu.VMEM((PASSAGES_HERE, LEN, PAIRS), BF16),
            pltpu.VMEM((16, half, B), BF16),
            pltpu.VMEM((16, half, B), BF16),
            pltpu.VMEM((12, half, B), BF16),
            pltpu.VMEM((12, half, B), BF16),
            pltpu.VMEM((2, half, B), BF16),
            pltpu.VMEM((2, half, B), BF16),
            pltpu.VMEM((12, half, B), BF16),
            pltpu.VMEM((12, half, B), BF16),
            pltpu.VMEM((2, half, B), BF16),
            pltpu.VMEM((2, half, B), BF16),
            pltpu.VMEM((2 * B, TQ), F32),
            pltpu.VMEM((2 * B, TQ), BF16),
            pltpu.VMEM((8, 2 * B // 8, TQ), BF16),
            pltpu.VMEM((2 * B // 8, TQ), BF16),
            pltpu.VMEM((8, 2 * B // 8, TQ), BF16),
            dma, dma((32,)), dma((2,)), dma((9,)),
            dma((15, 4)), dma((16, 4)),
            dma((8,)), dma((8,)),
            dma((16,)), dma((16,)),
            dma((12, 2)), dma((12, 2)), dma((2,)), dma((2,)),
            dma((12, 2)), dma((12, 2)), dma((2,)), dma((2,)),
            dma((8,)), dma((8,)), dma((8,)), dma((8,)),
        ],
        compiler_params=pltpu.CompilerParams(
            collective_id=0, has_side_effects=True, vmem_limit_bytes=60 * 2**20
        ),
        name="whole",
    )(lengths, owner, queries, grad_context, memory, w_key, w_value)
    gq, gm, gwk, gwv = pl.pallas_call(
        epilogue,
        out_shape=(
            jax.ShapeDtypeStruct((2 * TQ, B), BF16),
            jax.ShapeDtypeStruct((rows, B), BF16),
            jax.ShapeDtypeStruct((half, B), F32),
            jax.ShapeDtypeStruct((half, B), F32),
        ),
        in_specs=[vmem] * 3,
        out_specs=[vmem] * 4,
        name="turn",
    )(*outs)
    return gq, gm, gwk, gwv


def solution(mesh):
    in_specs = (
        P(None, "head"),
        P("psg", "head"),
        P("psg"),
        P("psg"),
        P(None, "head"),
        P(None, "head"),
        P(None, "head"),
    )
    out_specs = (P(None, "head"), P("psg", "head"), P("psg", "head"), P("psg", "head"))
    return jax.shard_map(
        on_device, mesh=mesh, in_specs=in_specs, out_specs=out_specs, check_vma=False
    )
```

profile of v0, /device:TPU:1, one launch (start us, length us, event | category | flops | bytes accessed | tf_op | source)
XLA Modules:
  0.0 95.0 jit_solution(6876107436479791806)
XLA Ops:
  0.6 91.4 %whole.1 = (bf16[8,64,128]{2,1,0:T(8,128)(2,1)}, bf16[1024,256]{1,0:T(8,128)(2,1)}, f32[4,256,256]{2,1,0:T(8,128)}) custom-call(s32[4]{0:T(128)} %len_ref.1, s32[4]{0:T(128)} %own_ref.1, bf16[256,256]{1,0:T(8,128)(2,1)} %q_in.1, bf16[256,256]{1,0:T(8,128)(2,1)} %c_in.1, bf16[1024,256]{1,0:T(8,128)(2,1)} %mem_ref.1, bf16[4096,256]{1,0:T(8,128)(2,1)} %wk_ref.1, ...), custom_call_target="tpu_custom_call" | custom-call | tf_op jit(solution)/shard_map/whole/pallas_call | solution.py:603
  92.1 2.9 %turn.1 = (bf16[256,256]{1,0:T(8,128)(2,1)}, bf16[1024,256]{1,0:T(8,128)(2,1)}, f32[512,256]{1,0:T(8,128)}, f32[512,256]{1,0:T(8,128)}) custom-call(bf16[8,64,128]{2,1,0:T(8,128)(2,1)} %get-tuple-element.7.gq_in, bf16[1024,256]{1,0:T(8,128)(2,1)} %get-tuple-element.8.gm_in, f32[4,256,256]{2,1,0:T(8,128)} %get-tuple-element.9.gw_in), custom_call_target="tpu_custom_call" | custom-call | tf_op jit(solution)/shard_map/turn/pallas_call | solution.py:661
where the time goes:
time: 95.1 us; the launch traced here: 95 us
  Pallas kernels  94.4 us (99%)
    pallas_call x1, Pallas kernels, on_device(): pl.pallas_call(kernel, out_shape=(jax.ShapeDtypeStruct((8, 2 * B // 8, TQ...  91.4 us
    pallas_call x1, Pallas kernels, on_device(): pl.pallas_call(epilogue, out_shape=(jax.ShapeDtypeStruct((2 * TQ, B), BF1...  2.93 us

commit v1 on v0

--- a/solution.py
+++ b/solution.py
@@ -42,7 +42,8 @@
 
 
 class Scatter:
-    def __init__(self, send, recv, ysend, yrecv, ssem, rsem, yssem, yrsem, following, before, partner):
+    def __init__(self, pair_first, send, recv, ysend, yrecv, ssem, rsem, yssem, yrsem, following, before, partner):
+        self.pair_first = pair_first
         self.send, self.recv, self.ysend, self.yrecv = send, recv, ysend, yrecv
         self.ssem, self.rsem, self.yssem, self.yrsem = ssem, rsem, yssem, yrsem
         self.following, self.before, self.partner = following, before, partner
@@ -57,6 +58,16 @@
             send_sem=self.ssem.at[index, way],
             recv_sem=self.rsem.at[index, way],
             device_id=self.before if way else self.following,
+            device_id_type=MESH,
+        )
+
+    def first_copy(self):
+        return pltpu.make_async_remote_copy(
+            src_ref=self.send.at[FIRST],
+            dst_ref=self.recv.at[FIRST],
+            send_sem=self.ssem.at[FIRST, 0],
+            recv_sem=self.rsem.at[FIRST, 0],
+            device_id=self.partner,
             device_id_type=MESH,
         )
 
@@ -93,10 +104,20 @@
                 self.ycopy(u).start()
             return
         index = first + "ABC".index(kind)
+        if self.pair_first and index == FIRST:
+            for way in (0, 1):
+                dz, r = chunk_of(kind, u, way)
+                self.send[index, way * B : (way + 1) * B, :] = own(dz, r, way).astype(BF16)
+            self.first_copy().start()
+            return
+        if self.pair_first and index == 0:
+            self.first_copy().wait_recv()
         for way in (0, 1):
             dz, r = chunk_of(kind, u, way)
             value = own(dz, r, way)
-            if kind == "C":
+            if self.pair_first and index == 0:
+                value = value + self.arrived(FIRST, way)
+            if kind == "C" and not (self.pair_first and first == FIRST):
                 self.copy(first, way).wait_recv()
                 value = value + self.arrived(first, way)
             self.send[index, way * B : (way + 1) * B, :] = value.astype(BF16)
@@ -104,6 +125,9 @@
 
     def finish(self, indices):
         for index in indices:
+            if self.pair_first and index == FIRST:
+                self.first_copy().wait_send()
+                continue
             for way in (0, 1):
                 self.copy(index, way).wait_send()
 
@@ -127,14 +151,15 @@
     ("C", 1, 1), ("A", 0, 0), ("B", 0, 0), ("D", 1, 1), ("C", 0, 0), ("A", 0, 1),
     ("B", 0, 1), ("C", 0, 1), ("D", 0, 0), ("D", 0, 1),
 )
+FIRST = 6
 LAST = (4, 5)
 EARLIER = tuple(index for index in range(12) if index not in LAST)
 
 
 def kernel(
-    len_ref, own_ref, q_in, c_in, mem_ref, wk_ref, wv_ref,
+    len_in, own_in, q_in, c_in, mem_ref, wk_ref, wv_ref,
     gq_out, gm_out, gw_out,
-    q_ref, c_ref, gm_own, gw_own, fm, w, qa, ca, qat, cat, acc, kt, e_ref, gp_ref, stat, sl, sall, g, gt, gs,
+    len_ref, own_ref, q_ref, c_ref, gm_own, gw_own, fm, w, qa, ca, qat, cat, acc, kt, e_ref, gp_ref, stat, sl, sall, g, gt, gs,
     sib_send, sib_recv, m_send, m_recv, my_send, my_recv, w_send, w_recv, wy_send, wy_recv,
     gq_acc, gq_send, gq_recv, gq_own, gq_full,
     mem_sem, w_sem, qc_sem, out_sem, ag_ssem, ag_rsem, st_ssem, st_rsem, sib_ssem, sib_rsem,
@@ -165,6 +190,8 @@
     q_copies = [
         pltpu.make_async_copy(q_in, q_ref, qc_sem.at[0]),
         pltpu.make_async_copy(c_in, c_ref, qc_sem.at[1]),
+        pltpu.make_async_copy(len_in, len_ref, qc_sem.at[2]),
+        pltpu.make_async_copy(own_in, own_ref, qc_sem.at[3]),
     ]
     for copy in q_copies:
         copy.start()
@@ -409,10 +436,10 @@
     lax.fori_loop(0, 2, gradients, 0)
 
     over_head = Scatter(
-        m_send, m_recv, my_send, my_recv, m_ssem, m_rsem, my_ssem, my_rsem, up, down, across
+        False, m_send, m_recv, my_send, my_recv, m_ssem, m_rsem, my_ssem, my_rsem, up, down, across
     )
     over_psg = Scatter(
-        w_send, w_recv, wy_send, wy_recv, w_ssem, w_rsem, wy_ssem, wy_rsem,
+        True, w_send, w_recv, wy_send, wy_recv, w_ssem, w_rsem, wy_ssem, wy_rsem,
         on_psg(0, 1), on_psg(0, 3), on_psg(1, 0),
     )
 
@@ -582,21 +609,37 @@
     out_copy(gq_full, gq_out, 8).wait()
 
 
-def epilogue(gq_in, gm_in, gw_in, gq_out, gm_out, gwk_out, gwv_out):
-    gm_out[...] = gm_in[...]
+def epilogue(gq_in, gm_in, gw_in, gq_out, gm_out, gwk_out, gwv_out, gq, gm, gw, gq_t, gw_t, sem):
+    def copy(source, target, number):
+        return pltpu.make_async_copy(source, target, sem.at[number])
+
+    def gw_write(r):
+        out = gwk_out if r < 2 else gwv_out
+        return copy(gw_t.at[r], out.at[pl.ds(r % 2 * B, B)], 6 + r)
+
+    reads = [copy(gw_in.at[r], gw.at[r], r) for r in range(4)]
+    reads += [copy(gm_in, gm, 4), copy(gq_in, gq, 5)]
+    writes = [gw_write(r) for r in range(4)]
+    writes += [copy(gm, gm_out, 10), copy(gq_t, gq_out, 11)]
+    for read in reads:
+        read.start()
     for r in range(4):
-        out = gwk_out if r < 2 else gwv_out
-        half = r % 2
-        out[half * B : (half + 1) * B, :] = gw_in[r].T
+        reads[r].wait()
+        gw_t[r] = gw[r].T
+        writes[r].start()
+    reads[4].wait()
+    writes[4].start()
+    reads[5].wait()
     for question in range(2):
-        turned = jnp.concatenate([gq_in[question * 4 + k] for k in range(4)], axis=0)
-        gq_out[question * TQ : (question + 1) * TQ, :] = turned.astype(F32).T.astype(BF16)
+        turned = jnp.concatenate([gq[question * 4 + k] for k in range(4)], axis=0)
+        gq_t[question * TQ : (question + 1) * TQ, :] = turned.astype(F32).T.astype(BF16)
+    writes[5].start()
+    for write in writes:
+        write.wait()
 
 
 def on_device(queries, memory, lengths, owner, w_key, w_value, grad_context):
     rows, width = memory.shape[0], w_key.shape[0]
-    vmem = pl.BlockSpec(memory_space=pltpu.VMEM)
-    smem = pl.BlockSpec(memory_space=pltpu.SMEM)
     anywhere = pl.BlockSpec(memory_space=pl.ANY)
     dma = pltpu.SemaphoreType.DMA
     half = 2 * B
@@ -607,9 +650,11 @@
             jax.ShapeDtypeStruct((rows, B), BF16),
             jax.ShapeDtypeStruct((4, B, B), F32),
         ),
-        in_specs=[smem, smem] + [anywhere] * 5,
+        in_specs=[anywhere] * 7,
         out_specs=[anywhere] * 3,
         scratch_shapes=[
+            pltpu.SMEM((PASSAGES_HERE,), jnp.int32),
+            pltpu.SMEM((PASSAGES_HERE,), jnp.int32),
             pltpu.VMEM((2 * TQ, B), BF16),
             pltpu.VMEM((2 * TQ, B), BF16),
             pltpu.VMEM((rows, B), BF16),
@@ -645,7 +690,7 @@
             pltpu.VMEM((8, 2 * B // 8, TQ), BF16),
             pltpu.VMEM((2 * B // 8, TQ), BF16),
             pltpu.VMEM((8, 2 * B // 8, TQ), BF16),
-            dma, dma((32,)), dma((2,)), dma((9,)),
+            dma, dma((32,)), dma((4,)), dma((9,)),
             dma((15, 4)), dma((16, 4)),
             dma((8,)), dma((8,)),
             dma((16,)), dma((16,)),
@@ -666,8 +711,16 @@
             jax.ShapeDtypeStruct((half, B), F32),
             jax.ShapeDtypeStruct((half, B), F32),
         ),
-        in_specs=[vmem] * 3,
-        out_specs=[vmem] * 4,
+        in_specs=[anywhere] * 3,
+        out_specs=[anywhere] * 4,
+        scratch_shapes=[
+            pltpu.VMEM((8, 2 * B // 8, TQ), BF16),
+            pltpu.VMEM((rows, B), BF16),
+            pltpu.VMEM((4, B, B), F32),
+            pltpu.VMEM((2 * TQ, B), BF16),
+            pltpu.VMEM((4, B, B), F32),
+            dma((12,)),
+        ],
         name="turn",
     )(*outs)
     return gq, gm, gwk, gwv

time: 95.1 us -> 93.1 us (0.979)
  Pallas kernels: 94.4 us -> 92.1 us
    pallas_call x1, Pallas kernels: 91.4 us -> 89.6 us  [on_device(): pl.pallas_call(kernel, out_shape=(jax.ShapeDtypeStruct((8, 2 * B // 8, TQ...]
where the time goes in v1:
time: 93.1 us; the launch traced here: 93 us
  Pallas kernels  92.1 us (99%)
    pallas_call x1, Pallas kernels, on_device(): pl.pallas_call(kernel, out_shape=(jax.ShapeDtypeStruct((8, 2 * B // 8, TQ...  89.6 us
    pallas_call x1, Pallas kernels, on_device(): pl.pallas_call(epilogue, out_shape=(jax.ShapeDtypeStruct((2 * TQ, B), BF1...  2.51 us

profile of v1, /device:TPU:1, one launch (start us, length us, event | category | flops | bytes accessed | tf_op | source)
XLA Modules:
  0.0 93.0 jit_solution(9929027338410307330)
XLA Ops:
  0.6 89.6 %whole.1 = (bf16[8,64,128]{2,1,0:T(8,128)(2,1)}, bf16[1024,256]{1,0:T(8,128)(2,1)}, f32[4,256,256]{2,1,0:T(8,128)}) custom-call(s32[4]{0:T(128)} %len_in.1, s32[4]{0:T(128)} %own_in.1, bf16[256,256]{1,0:T(8,128)(2,1)} %q_in.1, bf16[256,256]{1,0:T(8,128)(2,1)} %c_in.1, bf16[1024,256]{1,0:T(8,128)(2,1)} %mem_ref.1, bf16[4096,256]{1,0:T(8,128)(2,1)} %wk_ref.1, ...), custom_call_target="tpu_custom_call" | custom-call | tf_op jit(solution)/shard_map/whole/pallas_call | solution.py:646
  90.3 2.5 %turn.1 = (bf16[256,256]{1,0:T(8,128)(2,1)}, bf16[1024,256]{1,0:T(8,128)(2,1)}, f32[512,256]{1,0:T(8,128)}, f32[512,256]{1,0:T(8,128)}) custom-call(bf16[8,64,128]{2,1,0:T(8,128)(2,1)} %get-tuple-element.7.gq_in, bf16[1024,256]{1,0:T(8,128)(2,1)} %get-tuple-element.8.gm_in, f32[4,256,256]{2,1,0:T(8,128)} %get-tuple-element.9.gw_in), custom_call_target="tpu_custom_call" | custom-call | tf_op jit(solution)/shard_map/turn/pallas_call | solution.py:706

commit v2 on v1

--- a/solution.py
+++ b/solution.py
@@ -590,9 +590,13 @@
             over_head.finish(EARLIER)
             over_psg.finish(EARLIER)
         psg_item(number)
-        if number + 1 < len(ITEMS):
-            sibling_item(number + 1)
+        if number == 0:
+            sibling_item(1)
+        elif number + 2 < len(ITEMS):
+            sibling_item(number + 2)
         head_item(number)
+        if number == 0:
+            sibling_item(2)
         if number == 2:
             query_terms()
         if number == 8:

time: 93.1 us -> 93.2 us (level)
  no operation moved by 1% of the time
where the time goes in v2:
time: 93.2 us; the launch traced here: 92.5 us
  Pallas kernels  91.7 us (98%)
    pallas_call x1, Pallas kernels, on_device(): pl.pallas_call(kernel, out_shape=(jax.ShapeDtypeStruct((8, 2 * B // 8, TQ...  89.2 us
    pallas_call x1, Pallas kernels, on_device(): pl.pallas_call(epilogue, out_shape=(jax.ShapeDtypeStruct((2 * TQ, B), BF1...  2.51 us

profile of v2, /device:TPU:1, one launch (start us, length us, event | category | flops | bytes accessed | tf_op | source)
XLA Modules:
  0.0 92.5 jit_solution(12397172989074921857)
XLA Ops:
  0.6 89.2 %whole.1 = (bf16[8,64,128]{2,1,0:T(8,128)(2,1)}, bf16[1024,256]{1,0:T(8,128)(2,1)}, f32[4,256,256]{2,1,0:T(8,128)}) custom-call(s32[4]{0:T(128)} %len_in.1, s32[4]{0:T(128)} %own_in.1, bf16[256,256]{1,0:T(8,128)(2,1)} %q_in.1, bf16[256,256]{1,0:T(8,128)(2,1)} %c_in.1, bf16[1024,256]{1,0:T(8,128)(2,1)} %mem_ref.1, bf16[4096,256]{1,0:T(8,128)(2,1)} %wk_ref.1, ...), custom_call_target="tpu_custom_call" | custom-call | tf_op jit(solution)/shard_map/whole/pallas_call | solution.py:650
  89.8 2.5 %turn.1 = (bf16[256,256]{1,0:T(8,128)(2,1)}, bf16[1024,256]{1,0:T(8,128)(2,1)}, f32[512,256]{1,0:T(8,128)}, f32[512,256]{1,0:T(8,128)}) custom-call(bf16[8,64,128]{2,1,0:T(8,128)(2,1)} %get-tuple-element.7.gq_in, bf16[1024,256]{1,0:T(8,128)(2,1)} %get-tuple-element.8.gm_in, f32[4,256,256]{2,1,0:T(8,128)} %get-tuple-element.9.gw_in), custom_call_target="tpu_custom_call" | custom-call | tf_op jit(solution)/shard_map/turn/pallas_call | solution.py:710

commit v3 on v2

--- a/solution.py
+++ b/solution.py
@@ -436,7 +436,7 @@
     lax.fori_loop(0, 2, gradients, 0)
 
     over_head = Scatter(
-        False, m_send, m_recv, my_send, my_recv, m_ssem, m_rsem, my_ssem, my_rsem, up, down, across
+        True, m_send, m_recv, my_send, my_recv, m_ssem, m_rsem, my_ssem, my_rsem, up, down, across
     )
     over_psg = Scatter(
         True, w_send, w_recv, wy_send, wy_recv, w_ssem, w_rsem, wy_ssem, wy_rsem,

time: 93.2 us -> 94.5 us (1.014)
  Pallas kernels: 91.7 us -> 93.6 us
    pallas_call x1, Pallas kernels: 89.2 us -> 91.1 us  [on_device(): pl.pallas_call(kernel, out_shape=(jax.ShapeDtypeStruct((8, 2 * B // 8, TQ...]
where the time goes in v3:
time: 94.5 us; the launch traced here: 94.4 us
  Pallas kernels  93.6 us (99%)
    pallas_call x1, Pallas kernels, on_device(): pl.pallas_call(kernel, out_shape=(jax.ShapeDtypeStruct((8, 2 * B // 8, TQ...  91.1 us
    pallas_call x1, Pallas kernels, on_device(): pl.pallas_call(epilogue, out_shape=(jax.ShapeDtypeStruct((2 * TQ, B), BF1...  2.51 us

profile of v3, /device:TPU:1, one launch (start us, length us, event | category | flops | bytes accessed | tf_op | source)
XLA Modules:
  0.0 94.4 jit_solution(9020426848125837297)
XLA Ops:
  0.6 91.1 %whole.1 = (bf16[8,64,128]{2,1,0:T(8,128)(2,1)}, bf16[1024,256]{1,0:T(8,128)(2,1)}, f32[4,256,256]{2,1,0:T(8,128)}) custom-call(s32[4]{0:T(128)} %len_in.1, s32[4]{0:T(128)} %own_in.1, bf16[256,256]{1,0:T(8,128)(2,1)} %q_in.1, bf16[256,256]{1,0:T(8,128)(2,1)} %c_in.1, bf16[1024,256]{1,0:T(8,128)(2,1)} %mem_ref.1, bf16[4096,256]{1,0:T(8,128)(2,1)} %wk_ref.1, ...), custom_call_target="tpu_custom_call" | custom-call | tf_op jit(solution)/shard_map/whole/pallas_call | solution.py:650
  91.7 2.5 %turn.1 = (bf16[256,256]{1,0:T(8,128)(2,1)}, bf16[1024,256]{1,0:T(8,128)(2,1)}, f32[512,256]{1,0:T(8,128)}, f32[512,256]{1,0:T(8,128)}) custom-call(bf16[8,64,128]{2,1,0:T(8,128)(2,1)} %get-tuple-element.7.gq_in, bf16[1024,256]{1,0:T(8,128)(2,1)} %get-tuple-element.8.gm_in, f32[4,256,256]{2,1,0:T(8,128)} %get-tuple-element.9.gw_in), custom_call_target="tpu_custom_call" | custom-call | tf_op jit(solution)/shard_map/turn/pallas_call | solution.py:710

commit v4 on v2

--- a/solution.py
+++ b/solution.py
@@ -71,12 +71,12 @@
             device_id_type=MESH,
         )
 
-    def ycopy(self, u):
-        return pltpu.make_async_remote_copy(
-            src_ref=self.ysend.at[u],
-            dst_ref=self.yrecv.at[u],
-            send_sem=self.yssem.at[u],
-            recv_sem=self.yrsem.at[u],
+    def ycopy(self, u, way):
+        return pltpu.make_async_remote_copy(
+            src_ref=self.half(self.ysend, u, way),
+            dst_ref=self.half(self.yrecv, u, way),
+            send_sem=self.yssem.at[u, way],
+            recv_sem=self.yrsem.at[u, way],
             device_id=self.partner,
             device_id_type=MESH,
         )
@@ -89,19 +89,16 @@
         if kind == "D":
             mine = [own(0, way * 2 + u, way) for way in (0, 1)]
             for way in (0, 1):
-                self.copy(first + 1, way).wait_recv()
+                self.copy(first + 1, 1 - way).wait_recv()
                 self.copy(first + 2, way).wait_recv()
-            if dy == 0:
-                self.ycopy(u).wait_recv()
-            for way in (0, 1):
                 value = mine[way] + self.arrived(first + 2, way) + self.arrived(first + 1, 1 - way)
                 if dy == 1:
                     self.ysend[u, way * B : (way + 1) * B, :] = value.astype(BF16)
+                    self.ycopy(u, way).start()
                 else:
+                    self.ycopy(u, way).wait_recv()
                     value = value + self.yrecv[u, way * B : (way + 1) * B, :].astype(F32)
                     store(way * 2 + u, value)
-            if dy == 1:
-                self.ycopy(u).start()
             return
         index = first + "ABC".index(kind)
         if self.pair_first and index == FIRST:
@@ -133,7 +130,8 @@
 
     def finish_y(self):
         for u in (0, 1):
-            self.ycopy(u).wait_send()
+            for way in (0, 1):
+                self.ycopy(u, way).wait_send()
 
 
 def chunk_of(kind, u, way):
@@ -185,6 +183,11 @@
     up, down, across, sibling = on_head(0, 1), on_head(0, 3), on_head(1, 0), on_head(0, 0, 1)
     peers = [(k // 4, k % 4) for k in range(1, 8)]
 
+    barrier = pltpu.get_barrier_semaphore()
+    partners = [on_psg(*peer) for peer in reversed(peers)] + [across, up, down, sibling]
+    for device in partners:
+        pl.semaphore_signal(barrier, inc=1, device_id=device, device_id_type=MESH)
+
     mem_copy = pltpu.make_async_copy(mem_ref, fm.at[:, pl.ds(0, B)], mem_sem)
     mem_copy.start()
     q_copies = [
@@ -195,10 +198,6 @@
     ]
     for copy in q_copies:
         copy.start()
-    barrier = pltpu.get_barrier_semaphore()
-    partners = [on_psg(*peer) for peer in reversed(peers)] + [across, up, down, sibling]
-    for device in partners:
-        pl.semaphore_signal(barrier, inc=1, device_id=device, device_id_type=MESH)
     pl.semaphore_wait(barrier, len(partners))
 
     def block(slot, dc, r):
@@ -395,7 +394,7 @@
             device_id_type=MESH,
         )
 
-    for peer in peers:
+    for peer in reversed(peers):
         stat_copy(*peer).start()
     for peer in peers:
         stat_copy(*peer).wait_recv()
@@ -698,8 +697,8 @@
             dma((15, 4)), dma((16, 4)),
             dma((8,)), dma((8,)),
             dma((16,)), dma((16,)),
-            dma((12, 2)), dma((12, 2)), dma((2,)), dma((2,)),
-            dma((12, 2)), dma((12, 2)), dma((2,)), dma((2,)),
+            dma((12, 2)), dma((12, 2)), dma((2, 2)), dma((2, 2)),
+            dma((12, 2)), dma((12, 2)), dma((2, 2)), dma((2, 2)),
             dma((8,)), dma((8,)), dma((8,)), dma((8,)),
         ],
         compiler_params=pltpu.CompilerParams(

time: 93.2 us -> 93.7 us (level)
  Pallas kernels: 91.7 us -> 92.8 us
    pallas_call x1, Pallas kernels: 89.2 us -> 90.3 us  [on_device(): pl.pallas_call(kernel, out_shape=(jax.ShapeDtypeStruct((8, 2 * B // 8, TQ...]
where the time goes in v4:
time: 93.7 us; the launch traced here: 93.6 us
  Pallas kernels  92.8 us (99%)
    pallas_call x1, Pallas kernels, on_device(): pl.pallas_call(kernel, out_shape=(jax.ShapeDtypeStruct((8, 2 * B // 8, TQ...  90.3 us
    pallas_call x1, Pallas kernels, on_device(): pl.pallas_call(epilogue, out_shape=(jax.ShapeDtypeStruct((2 * TQ, B), BF1...  2.51 us

profile of v4, /device:TPU:1, one launch (start us, length us, event | category | flops | bytes accessed | tf_op | source)
XLA Modules:
  0.0 93.6 jit_solution(15915786500087830629)
XLA Ops:
  0.6 90.3 %whole.1 = (bf16[8,64,128]{2,1,0:T(8,128)(2,1)}, bf16[1024,256]{1,0:T(8,128)(2,1)}, f32[4,256,256]{2,1,0:T(8,128)}) custom-call(s32[4]{0:T(128)} %len_in.1, s32[4]{0:T(128)} %own_in.1, bf16[256,256]{1,0:T(8,128)(2,1)} %q_in.1, bf16[256,256]{1,0:T(8,128)(2,1)} %c_in.1, bf16[1024,256]{1,0:T(8,128)(2,1)} %mem_ref.1, bf16[4096,256]{1,0:T(8,128)(2,1)} %wk_ref.1, ...), custom_call_target="tpu_custom_call" | custom-call | tf_op jit(solution)/shard_map/whole/pallas_call | solution.py:649
  90.9 2.5 %turn.1 = (bf16[256,256]{1,0:T(8,128)(2,1)}, bf16[1024,256]{1,0:T(8,128)(2,1)}, f32[512,256]{1,0:T(8,128)}, f32[512,256]{1,0:T(8,128)}) custom-call(bf16[8,64,128]{2,1,0:T(8,128)(2,1)} %get-tuple-element.7.gq_in, bf16[1024,256]{1,0:T(8,128)(2,1)} %get-tuple-element.8.gm_in, f32[4,256,256]{2,1,0:T(8,128)} %get-tuple-element.9.gw_in), custom_call_target="tpu_custom_call" | custom-call | tf_op jit(solution)/shard_map/turn/pallas_call | solution.py:709
